TPU v7x, 256 devices: a whole 4x4x8 slice. The times are simulated.
256 devices in a mesh: grp: 8 (over z), shard: 32 (over y, x, core).
Axes of the slice: x: 4, y: 4, z: 8, core: 2. Of those that a mesh axis runs over, the one named last changes fastest.
Arguments:
- activations: bfloat16 [32768, 8192], P('grp', 'shard'), may hold values from -6 to 6
- cotangent: bfloat16 [32768, 28672], P('grp', 'shard'), may hold values from -0.29882812 to 0.29882812
- adapter_down_matrices: bfloat16 [64, 16, 8192], P('grp', None, 'shard'), may hold values from -0.0625 to 0.0625
- adapter_up_weight: bfloat16 [64, 16, 28672], P('grp', None, 'shard'), may hold values from -0.03125 to 0.03125
- down_feedback_residual: float32 [64, 16, 8192], P('grp', None, 'shard'), may hold values from -3 to 3
- up_feedback_residual: float32 [64, 16, 28672], P('grp', None, 'shard'), may hold values from -3 to 3
- group_tenant_adapters: int32 [8, 8], replicated, may hold values from 0 to 63, as said below
- adapter_owner_slot: int32 [64], replicated, may hold values from 0 to 63, as said below
- block_list_entry: int32 [128], P('grp'), may hold values from 0 to 7
- block_token_rows: int32 [128], P('grp'), may hold values from 1 to 256, as said below
Outputs:
- grad_down: float32 [64, 16, 8192], P('grp', None, 'shard')
- grad_up: float32 [64, 16, 28672], P('grp', None, 'shard')
Inputs may be any that keep to these rules, and one draw needn't show every extreme that they name: adapter_owner_slot is a permutation. `group_tenant_adapters`: each row names 8 different adapters; at most 2 entries of a row lie with one owner group, and one owner group holds exactly 2 entries of every row. `block_token_rows`: some block of every draw is full.
All inputs are finite; a program needn't handle non-finite values.
Results may differ from a plain program's by a relative error of at most 0.0028.
Values may be sent and summed in bfloat16 or wider, within the bound.
A program may use at most 64 MiB of HBM per device.

v0:
```python
import jax
import jax.numpy as jnp
from jax import lax
from jax.sharding import PartitionSpec as P

adapter_scale = 2.0


def local(
    activations,
    cotangent,
    adapter_down_matrices,
    adapter_up_weight,
    down_feedback_residual,
    up_feedback_residual,
    group_tenant_adapters,
    adapter_owner_slot,
    block_list_entry,
    block_token_rows,
):
    groups = lax.axis_size("grp")
    my_group = lax.axis_index("grp")
    slots_per_owner = adapter_down_matrices.shape[0]
    listed = group_tenant_adapters.shape[1]
    token_block_list = block_list_entry.shape[0]
    block_length = activations.shape[0] // token_block_list
    width_down = activations.shape[1]
    width_up = cotangent.shape[1]
    bf16 = jnp.bfloat16
    single_precision_float = jnp.float32
    highest_precision = lax.Precision.HIGHEST
    match = (
        group_tenant_adapters[:, :, None]
        == jnp.arange(adapter_owner_slot.shape[0], dtype=jnp.int32)[None, None, :]
    )
    slots = jnp.sum(jnp.where(match, adapter_owner_slot[None, None, :], 0), axis=2)
    group_index = jnp.arange(groups, dtype=jnp.int32)
    mine = (group_index == my_group)[:, None]
    own_slots = jnp.sum(jnp.where(mine, slots, 0), axis=0)
    pick_mask = own_slots[:, None] == jnp.arange(groups * slots_per_owner, dtype=jnp.int32)[None, :]
    pick = pick_mask.astype(bf16)
    pick_float = pick_mask.astype(single_precision_float)
    every_down, every_up = (
        lax.all_gather(adapter_down_matrices, "grp", axis=0, tiled=True),
        lax.all_gather(adapter_up_weight, "grp", axis=0, tiled=True),
    )
    list_down = jnp.einsum(
        "es,srd->erd", pick, every_down, preferred_element_type=single_precision_float
    ).astype(bf16)
    list_up = jnp.einsum(
        "es,srf->erf", pick, every_up, preferred_element_type=single_precision_float
    ).astype(bf16)
    entry_hot = block_list_entry[:, None] == jnp.arange(listed, dtype=jnp.int32)[None, :]
    input_token_rows = activations.reshape(token_block_list, block_length, width_down)
    upstream = cotangent.reshape(token_block_list, block_length, width_up)
    hot_table = entry_hot.astype(bf16)
    down_block_gradients = jnp.einsum(
        "be,erd->brd", hot_table, list_down, preferred_element_type=single_precision_float
    ).astype(bf16)
    up_block_grads = jnp.einsum(
        "be,erf->brf", hot_table, list_up, preferred_element_type=single_precision_float
    ).astype(bf16)
    part_in = jnp.einsum(
        "wyc,wmc->wym",
        down_block_gradients,
        input_token_rows,
        preferred_element_type=single_precision_float,
    )
    part_back = jnp.einsum(
        "brf,bkf->brk", up_block_grads, upstream, preferred_element_type=single_precision_float
    )
    rank_input, low_back = lax.psum((part_in, part_back), "shard")
    valid_token_mask = (
        jnp.arange(block_length, dtype=jnp.int32)[None, :] < block_token_rows[:, None]
    ).astype(single_precision_float)
    frozen_weight = adapter_scale * valid_token_mask[:, None, :]
    scaled_in = (rank_input * frozen_weight).astype(bf16)
    scaled_backward = (low_back * frozen_weight).astype(bf16)
    block_up = jnp.einsum(
        "brk,bkf->brf", scaled_in, upstream, preferred_element_type=single_precision_float
    )
    block_down_gradient = jnp.einsum(
        "sli,sit->slt",
        scaled_backward,
        input_token_rows,
        preferred_element_type=single_precision_float,
    )
    hot_float = entry_hot.astype(single_precision_float)
    step_up = jnp.einsum("be,brf->erf", hot_float, block_up, precision=highest_precision)
    step_down = jnp.einsum(
        "be,brd->erd", hot_float, block_down_gradient, precision=highest_precision
    )
    sent_down = step_down + down_feedback_residual
    sent_up = step_up + up_feedback_residual
    dense_down = jnp.einsum("es,erd->srd", pick_float, sent_down, precision=highest_precision)
    dense_up = jnp.einsum("es,erf->srf", pick_float, sent_up, precision=highest_precision)
    grad_down, grad_up = (
        lax.psum_scatter(dense_down, "grp", scatter_dimension=0, tiled=True),
        lax.psum_scatter(dense_up, "grp", scatter_dimension=0, tiled=True),
    )
    return (grad_down, grad_up)


def solution(mesh):
    in_specs = (
        P("grp", "shard"),
        P("grp", "shard"),
        P("grp", None, "shard"),
        P("grp", None, "shard"),
        P("grp", None, "shard"),
        P("grp", None, "shard"),
        P(),
        P(),
        P("grp"),
        P("grp"),
    )
    out_specs = (P("grp", None, "shard"), P("grp", None, "shard"))
    return jax.shard_map(local, mesh=mesh, in_specs=in_specs, out_specs=out_specs, check_vma=False)
```

profile of v0, /device:TPU:1, one launch (start us, length us, event | category | flops | bytes accessed | tf_op | source)
XLA Modules:
  0.0 277.3 jit_solution(8853237004398565497)
XLA Ops:
  7.2 0.7 all-gather.2.cloned.1.call-update
  7.9 0.0 all-reduce.3.cloned.1.call-start
  8.0 1.0 select_reduce_fusion
  9.0 0.1 select_reduce_fusion.1
  9.1 25.1 %all_gather.7 = bf16[64,16,256]{2,1,0:T(8,128)(2,1)S(1)} all-gather(bf16[8,16,256]{2,1,0:T(8,128)(2,1)} %param.12), channel_id=1, replica_groups=mesh['grp'=8,'shard'=32] {'grp'}, dimensions={0}, use_global_device_ids=true | all-gather | bytes 589824 | tf_op jit(solution)/shard_map/all_gather | solution.py:44
  34.1 1.0 convolution_convert_fusion.1
  35.2 1.4 fusion.15
  36.5 15.0 %all-gather.2.cloned.1.call-done = bf16[64,16,896]{2,1,0:T(8,128)(2,1)} async-done(((bf16[8,16,896]{2,1,0:T(8,128)(2,1)}), bf16[64,16,896]{2,1,0:T(8,128)(2,1)}) %all-gather.2.cloned.1.call-update) | async-done | bytes 1835024 | tf_op jit(solution)/shard_map/all_gather | solution.py:45
  51.6 2.1 convolution_convert_fusion
  53.7 5.8 %fusion.10 = f32[16,16,256]{2,1,0:T(8,128)} fusion(bf16[16,256,896]{2,1,0:T(8,128)(2,1)} %bitcast.24, bf16[16,16,896]{2,0,1:T(8,128)(2,1)S(1)} %convolution_convert_fusion), kind=kOutput, calls=%fused_computation.10 | convolution fusion | flops 117440512 | bytes 8060928 | tf_op jit(solution)/shard_map/brf,bkf->brk/dot_general | solution.py:69
  59.5 0.0 reduce-scatter.3.cloned.1.call-start
  59.6 0.1 fusion.19
  59.7 115.6 %all-reduce.3.cloned.1.call-done = (f32[16,16,256]{2,1,0:T(8,128)}, f32[16,16,256]{2,1,0:T(8,128)}) async-done(((f32[16,16,256]{2,1,0:T(8,128)}, f32[16,16,256]{2,1,0:T(8,128)}), (f32[16,16,256]{2,1,0:T(8,128)}, f32[16,16,256]{2,1,0:T(8,128)})) %all-reduce.3.cloned.1.call-update) | async-done | bytes 524304 | tf_op jit(solution)/shard_map/psum | solution.py:72
  175.3 1.4 fusion.13
  176.6 0.4 convolution_add_fusion.1
  177.0 1.7 fusion.25
  178.7 0.0 reduce-scatter.5.cloned.1.call-start
  178.8 4.2 %fusion.14 = f32[16,16,896]{2,1,0:T(8,128)S(1)} fusion(bf16[16,256,896]{2,1,0:T(8,128)(2,1)} %bitcast.25, f32[16,16,256]{2,1,0:T(8,128)S(1)} %copy-done.1, f32[16,256]{1,0:T(8,128)S(1)} %fusion.19), kind=kOutput, calls=%fused_computation.16 | convolution fusion | flops 117571584 | bytes 8536064 | tf_op jit(solution)/shard_map/brk,bkf->brf/dot_general | solution.py:79
  183.0 0.8 convolution_add_fusion
  183.8 3.5 %fusion.21 = f32[64,16,896]{2,0,1:T(8,128)} fusion(f32[8,16,896]{2,0,1:T(8,128)S(1)} %convolution_add_fusion, s32[8]{0:T(128)S(1)} %select_reduce_fusion.1), kind=kOutput, calls=%fused_computation.29 | convolution fusion | flops 88080896 | bytes 4128800 | tf_op jit(solution)/shard_map/es,erf->srf/dot_general | solution.py:96
  187.3 25.0 %reduce-scatter.3.cloned.1.call-done = f32[8,16,256]{2,0,1:T(8,128)} async-done(((f32[64,16,256]{2,0,1:T(8,128)}), f32[8,16,256]{2,0,1:T(8,128)}) %reduce-scatter.3.cloned.1.call-update) | async-done | bytes 131088 | tf_op jit(solution)/shard_map/reduce_scatter | solution.py:98
  212.3 1.6 copy.28
  213.9 55.0 %reduce-scatter.5.cloned.1.call-done = f32[8,16,896]{2,0,1:T(8,128)} async-done(((f32[64,16,896]{2,0,1:T(8,128)}), f32[8,16,896]{2,0,1:T(8,128)}) %reduce-scatter.5.cloned.1.call-update) | async-done | bytes 458768 | tf_op jit(solution)/shard_map/reduce_scatter | solution.py:99
  268.9 1.9 copy.29
  (17 shorter events, 0.1 us)
Async XLA Ops:
  7.2 28.0 %copy-start = (bf16[4096,256]{1,0:T(8,128)(2,1)S(1)}, bf16[4096,256]{1,0:T(8,128)(2,1)}, u32[]{:S(2)}) copy-start(bf16[4096,256]{1,0:T(8,128)(2,1)} %param.10) | copy-start | bytes 6291460
  7.2 44.4 %copy-start.4 = (s32[16]{0:T(128)S(1)}, s32[16]{0:T(128)}, u32[]{:S(2)}) copy-start(s32[16]{0:T(128)} %param.18) | copy-start | bytes 196
  7.2 44.4 %all-gather.2.cloned.1.call-start = ((), (), s32[]{:S(2)}) async-start(), calls=%async_computation.2 | async-start | bytes 2064384 | tf_op jit(solution)/shard_map/all_gather | solution.py:45
  7.9 167.3 %all-reduce.3.cloned.1.call-start = ((), (), s32[]{:S(2)}) async-start(), calls=%async_computation.5 | async-start | bytes 1048576 | tf_op jit(solution)/shard_map/psum | solution.py:72
  53.7 5.9 %copy-start.5 = (s32[16]{0:T(128)S(1)}, s32[16]{0:T(128)}, u32[]{:S(2)}) copy-start(s32[16]{0:T(128)} %param.19) | copy-start | bytes 196
  59.5 117.1 %copy-start.3 = (f32[8,16,256]{2,1,0:T(8,128)S(1)}, f32[8,16,256]{2,1,0:T(8,128)}, u32[]{:S(2)}) copy-start(f32[8,16,256]{2,1,0:T(8,128)} %param.14) | copy-start | bytes 393220
  59.5 152.7 %reduce-scatter.3.cloned.1.call-start = ((), (), s32[]{:S(2)}) async-start(), calls=%async_computation.3 | async-start | bytes 1179648 | tf_op jit(solution)/shard_map/reduce_scatter | solution.py:98
  175.3 3.5 %copy-start.1 = (f32[16,16,256]{2,1,0:T(8,128)S(1)}, f32[16,16,256]{2,1,0:T(8,128)}, u32[]{:S(2)}) copy-start(f32[16,16,256]{2,1,0:T(8,128)} %get-tuple-element.9) | copy-start | bytes 786436
  178.7 90.2 %reduce-scatter.5.cloned.1.call-start = ((), (), s32[]{:S(2)}) async-start(), calls=%async_computation.4 | async-start | bytes 4128768 | tf_op jit(solution)/shard_map/reduce_scatter | solution.py:99
  178.8 4.2 %copy-start.2 = (f32[8,16,896]{2,1,0:T(8,128)S(1)}, f32[8,16,896]{2,1,0:T(8,128)}, u32[]{:S(2)}) copy-start(f32[8,16,896]{2,1,0:T(8,128)} %param.15) | copy-start | bytes 1376260
Sparse Core Ops, SparseCore 0:
  9.8 41.7 all-gather.1
  59.6 115.5 all-reduce.2
  178.8 33.3 reduce-scatter.2
  214.8 53.9 reduce-scatter.4
where the time goes:
time: 278 us; the launch traced here: 277 us
  waiting for transfers between devices  211 us (76%)
  blocking collectives  25.1 us (9%)
  matrix products  22.2 us (8%)
  between operations  13.9 us (5%)
  local copies, waits for them, and re-layouts  3.51 us (1%)
    psum x1, waiting for transfers between devices, local(): rank_input, low_back = lax.psum((part_in, part_back), 'shard')  116 us
    reduce_scatter x1, waiting for transfers between devices, local(): lax.psum_scatter(dense_up, 'grp', scatter_dimension=0, tiled=True)  55 us
    all_gather x1, blocking collectives, local(): lax.all_gather(adapter_down_matrices, 'grp', axis=0, tiled=True)  25.1 us
    reduce_scatter x1, waiting for transfers between devices, local(): lax.psum_scatter(dense_down, 'grp', scatter_dimension=0, tiled=True)  25 us
    all_gather x1, waiting for transfers between devices, local(): lax.all_gather(adapter_up_weight, 'grp', axis=0, tiled=True)  15 us
    dot_general x1, matrix products, local(): jnp.einsum('brf,bkf->brk', up_block_grads, upstream, preferred_element_ty...  5.83 us
  transfers between devices with their start and end apart: 4, of which 4 were waited for; matrix products, arithmetic and copies ran while one was open for 5% of the time, Pallas kernels for 0%

commit v1 on v0

v1 whole, which is shorter than its diff:
```python
import functools

import jax
import jax.numpy as jnp
from jax import lax
from jax.experimental import pallas as pl
from jax.experimental.pallas import tpu as pltpu
from jax.sharding import PartitionSpec as P

MESH = pl.DeviceIdType.MESH
bf16, f32, i32 = jnp.bfloat16, jnp.float32, jnp.int32
adapter_scale = 2.0


def kernel(
    groups,
    shards,
    x_hbm,
    c_hbm,
    ad_hbm,
    au_hbm,
    rd_hbm,
    ru_hbm,
    lists,
    slot_of,
    entry_of,
    rows_of,
    gd_hbm,
    gu_hbm,
    x,
    c,
    ad,
    au,
    rd,
    ru,
    ad_out,
    au_out,
    ad_in,
    au_in,
    part_x,
    part_c,
    rs_x,
    rs_c,
    ag_x,
    ag_c,
    spread,
    acc_d,
    acc_u,
    gd_out,
    gu_out,
    gd_in,
    gu_in,
    gd,
    gu,
    slot_tab,
    entry_tab,
    place_tab,
    load_sem,
    ad_send,
    ad_recv,
    au_send,
    au_recv,
    xy_send,
    xy_recv,
    gd_send,
    gd_recv,
    gu_send,
    gu_recv,
    store_sem,
):
    chips = shards // 2
    per_owner, rank, _ = ad.shape
    listed = rd.shape[0]
    block = x.shape[0] // chips
    half = block // 2
    me = lax.axis_index("grp")
    sh = lax.axis_index("shard")
    chip, core = lax.div(sh, 2), lax.rem(sh, 2)
    order = sorted(range(1, groups), key=lambda d: -min(d, groups - d))

    def group_at(d):
        return lax.rem(me + d, groups)

    loads = [
        pltpu.make_async_copy(src, dst, load_sem.at[i])
        for i, (src, dst) in enumerate(
            ((ad_hbm, ad), (au_hbm, au), (x_hbm, x), (c_hbm, c), (rd_hbm, rd), (ru_hbm, ru))
        )
    ]
    for load in loads:
        load.start()

    barrier = pltpu.get_barrier_semaphore()
    for d in range(1, groups):
        pl.semaphore_signal(barrier, inc=1, device_id=(group_at(d), sh), device_id_type=MESH)

    def greet(d, _):
        pl.semaphore_signal(
            barrier, inc=1, device_id=(me, lax.rem(sh + d, shards)), device_id_type=MESH
        )
        return _

    lax.fori_loop(1, shards, greet, 0)

    firsts = []
    for d in range(groups):
        row = group_at(d)
        first, second = i32(-1), i32(-1)
        for e in range(listed):
            s = slot_of[lists[row, e]]
            mine = lax.div(s, i32(per_owner)) == me
            at = lax.rem(s, i32(per_owner))
            second = jnp.where(mine & (first >= 0), at, second)
            first = jnp.where(mine & (first < 0), at, first)
        slot_tab[2 * d] = first
        slot_tab[2 * d + 1] = second
        firsts.append((jnp.maximum(first, 0), jnp.maximum(second, 0)))

    loads[0].wait()
    loads[1].wait()
    for d in range(groups):
        for k in range(2):
            if d:
                ad_out[d - 1, k] = ad[firsts[d][k]]
                au_out[d - 1, k] = au[firsts[d][k]]
            else:
                ad_in[2 * me + k] = ad[firsts[d][k]]
                au_in[2 * me + k] = au[firsts[d][k]]

    pl.semaphore_wait(barrier, groups - 1 + shards - 1)

    for out, into, send, recv in ((ad_out, ad_in, ad_send, ad_recv), (au_out, au_in, au_send, au_recv)):
        for d in order:
            pltpu.make_async_remote_copy(
                src_ref=out.at[d - 1],
                dst_ref=into.at[pl.ds(2 * me, 2)],
                send_sem=send,
                recv_sem=recv,
                device_id=(group_at(d), sh),
                device_id_type=MESH,
            ).start()

    owners = []
    for e in range(listed):
        owners.append(lax.div(slot_of[lists[me, e]], i32(per_owner)))
    places = []
    for e in range(listed):
        k = i32(0)
        for before in range(e):
            k = k + jnp.where(owners[before] == owners[e], 1, 0)
        places.append(2 * owners[e] + k)
        place_tab[e] = places[e]
    for p in range(2 * groups):
        found = i32(0)
        for e in range(listed):
            found = jnp.where(places[e] == p, e, found)
        entry_tab[p] = found

    def all_bytes(ref, sem):
        pltpu.make_async_copy(ref, ref, sem).wait()

    def low_rank(tokens, adapters, part, rs, ag, which):
        send, recv = xy_send.at[2 * which], xy_recv.at[2 * which]

        def project(i):
            b = lax.rem(chip + i, chips)
            low = lax.dot_general(
                adapters[place_tab[entry_of[b]]],
                tokens[pl.ds(pl.multiple_of(b * block, block), block), :],
                (((1,), (1,)), ((), ())),
                preferred_element_type=f32,
            )
            part[b, 0] = low[:, :half]
            part[b, 1] = low[:, half:]
            return b

        def send_part(b, k, slot):
            pltpu.make_async_remote_copy(
                src_ref=part.at[b, k],
                dst_ref=rs.at[slot],
                send_sem=send,
                recv_sem=recv,
                device_id=(me, 2 * b + k),
                device_id_type=MESH,
            ).start()

        step = 3 if (chips - 1) % 3 == 0 else 1

        def some(j, _):
            first = 1 + j * step
            at = [project(first + t) for t in range(step)]
            for t in range(step):
                for k in range(2):
                    send_part(at[t], k, 2 * (first + t - 1) + core)
            return _

        lax.fori_loop(0, (chips - 1) // step, some, 0)
        project(0)
        send_part(chip, 1 - core, shards - 2)
        all_bytes(rs, recv)

        low = part[chip, core] + jnp.sum(rs[...], axis=0)
        token = core * half + lax.broadcasted_iota(i32, (rank, half), 1)
        scale = jnp.where(token < rows_of[chip], adapter_scale, 0.0)
        ag[sh] = (low * scale).astype(bf16)

        send, recv = xy_send.at[2 * which + 1], xy_recv.at[2 * which + 1]

        def give(b, k):
            pltpu.make_async_remote_copy(
                src_ref=ag.at[sh],
                dst_ref=ag.at[sh],
                send_sem=send,
                recv_sem=recv,
                device_id=(me, 2 * b + k),
                device_id_type=MESH,
            ).start()

        def give_chip(i, _):
            b = lax.rem(chip + i, chips)
            give(b, 0)
            give(b, 1)
            return _

        lax.fori_loop(1, chips, give_chip, 0)
        give(chip, 1 - core)
        all_bytes(ag.at[pl.ds(0, shards - 1)], recv)

    def gradient(ag, tokens, residual, acc):
        def place(b, _):
            e = entry_of[b]
            for h in range(2):
                columns = pl.ds(pl.multiple_of(b * block + h * half, half), half)
                v = ag[2 * b + h]
                for l in range(listed):
                    spread[l * rank : (l + 1) * rank, columns] = jnp.where(e == l, v, jnp.zeros_like(v))
            return _

        lax.fori_loop(0, chips, place, 0)
        width = tokens.shape[1]
        for start in range(0, width, 256):
            stop = min(start + 256, width)
            step = jnp.dot(spread[...], tokens[:, start:stop], preferred_element_type=f32)
            acc[:, :, start:stop] = step.reshape(listed, rank, stop - start) + residual[:, :, start:stop]

    def send_gradient(acc, out, into, send, recv):
        for d in order:
            owner = group_at(d)
            for k in range(2):
                out[d - 1, k] = acc[entry_tab[2 * owner + k]].astype(bf16)
            pltpu.make_async_remote_copy(
                src_ref=out.at[d - 1],
                dst_ref=into.at[d - 1],
                send_sem=send,
                recv_sem=recv.at[d - 1],
                device_id=(owner, sh),
                device_id_type=MESH,
            ).start()

    def collect(acc, into, recv, total):
        values = [acc[entry_tab[2 * me + k]] for k in range(2)]
        for s in range(per_owner):
            total[s] = jnp.where(slot_tab[0] == s, values[0], 0.0) + jnp.where(
                slot_tab[1] == s, values[1], 0.0
            )
        for d in reversed(order):
            all_bytes(into.at[d - 1], recv.at[d - 1])
            values = [into[d - 1, k].astype(f32) for k in range(2)]
            at = [slot_tab[2 * (groups - d) + k] for k in range(2)]
            for s in range(per_owner):
                total[s] += jnp.where(at[0] == s, values[0], 0.0) + jnp.where(
                    at[1] == s, values[1], 0.0
                )

    loads[2].wait()
    all_bytes(ad_in.at[pl.ds(0, 2 * groups - 2)], ad_recv)
    low_rank(x, ad_in, part_x, rs_x, ag_x, 0)
    loads[3].wait()
    loads[5].wait()
    gradient(ag_x, c, ru, acc_u)
    send_gradient(acc_u, gu_out, gu_in, gu_send, gu_recv)

    all_bytes(au_in.at[pl.ds(0, 2 * groups - 2)], au_recv)
    low_rank(c, au_in, part_c, rs_c, ag_c, 1)
    loads[4].wait()
    gradient(ag_c, x, rd, acc_d)
    send_gradient(acc_d, gd_out, gd_in, gd_send, gd_recv)

    collect(acc_u, gu_in, gu_recv, gu)
    store_u = pltpu.make_async_copy(gu, gu_hbm, store_sem.at[0])
    store_u.start()
    collect(acc_d, gd_in, gd_recv, gd)
    store_d = pltpu.make_async_copy(gd, gd_hbm, store_sem.at[1])
    store_d.start()

    all_bytes(ad_out, ad_send)
    all_bytes(au_out, au_send)
    all_bytes(rs_x, xy_send.at[0])
    all_bytes(ag_x.at[pl.ds(0, shards - 1)], xy_send.at[1])
    all_bytes(rs_c, xy_send.at[2])
    all_bytes(ag_c.at[pl.ds(0, shards - 1)], xy_send.at[3])
    all_bytes(gu_out, gu_send)
    all_bytes(gd_out, gd_send)
    store_u.wait()
    store_d.wait()


def solution(mesh):
    groups, shards = mesh.shape["grp"], mesh.shape["shard"]

    def local(x, c, ad, au, rd, ru, lists, slot_of, entry_of, rows_of):
        tokens, wd = x.shape
        wu = c.shape[1]
        per_owner, rank, _ = ad.shape
        listed = lists.shape[1]
        chips = shards // 2
        half = tokens // chips // 2
        vmem, dma = pltpu.VMEM, pltpu.SemaphoreType.DMA
        places = 2 * groups
        return pl.pallas_call(
            functools.partial(kernel, groups, shards),
            out_shape=(
                jax.ShapeDtypeStruct((per_owner, rank, wd), f32),
                jax.ShapeDtypeStruct((per_owner, rank, wu), f32),
            ),
            in_specs=[pl.BlockSpec(memory_space=pltpu.HBM)] * 6
            + [pl.BlockSpec(memory_space=pltpu.SMEM)] * 4,
            out_specs=[pl.BlockSpec(memory_space=pltpu.HBM)] * 2,
            scratch_shapes=[
                vmem((tokens, wd), bf16),
                vmem((tokens, wu), bf16),
                vmem((per_owner, rank, wd), bf16),
                vmem((per_owner, rank, wu), bf16),
                vmem((listed, rank, wd), f32),
                vmem((listed, rank, wu), f32),
                vmem((groups - 1, 2, rank, wd), bf16),
                vmem((groups - 1, 2, rank, wu), bf16),
                vmem((places, rank, wd), bf16),
                vmem((places, rank, wu), bf16),
                vmem((chips, 2, rank, half), f32),
                vmem((chips, 2, rank, half), f32),
                vmem((shards - 1, rank, half), f32),
                vmem((shards - 1, rank, half), f32),
                vmem((shards, rank, half), bf16),
                vmem((shards, rank, half), bf16),
                vmem((listed * rank, tokens), bf16),
                vmem((listed, rank, wd), f32),
                vmem((listed, rank, wu), f32),
                vmem((groups - 1, 2, rank, wd), bf16),
                vmem((groups - 1, 2, rank, wu), bf16),
                vmem((groups - 1, 2, rank, wd), bf16),
                vmem((groups - 1, 2, rank, wu), bf16),
                vmem((per_owner, rank, wd), f32),
                vmem((per_owner, rank, wu), f32),
                pltpu.SMEM((places,), i32),
                pltpu.SMEM((places,), i32),
                pltpu.SMEM((listed,), i32),
                dma((6,)),
                dma,
                dma,
                dma,
                dma,
                dma((4,)),
                dma((4,)),
                dma,
                dma((groups - 1,)),
                dma,
                dma((groups - 1,)),
                dma((2,)),
            ],
            compiler_params=pltpu.CompilerParams(
                collective_id=0, has_side_effects=True, vmem_limit_bytes=56 * 2**20
            ),
        )(x, c, ad, au, rd, ru, lists, slot_of, entry_of, rows_of)

    split = P("grp", None, "shard")
    return jax.shard_map(
        local,
        mesh=mesh,
        in_specs=(P("grp", "shard"),) * 2 + (split,) * 4 + (P(), P(), P("grp"), P("grp")),
        out_specs=(split, split),
        check_vma=False,
    )
```

time: 278 us -> 55.2 us (0.20)
  waiting for transfers between devices: 211 us -> 0 us
  Pallas kernels: 0 us -> 51 us
  blocking collectives: 25.1 us -> 0 us
  matrix products: 22.2 us -> 0 us
  between operations: 13.9 us -> 0.64 us
    psum x1 -> x0, waiting for transfers between devices: 116 us -> none  [local(): rank_input, low_back = lax.psum((part_in, part_back), 'shard')]
    reduce_scatter x2 -> x0, waiting for transfers between devices: 80 us -> none  [the longest x1 55 us: local(): lax.psum_scatter(dense_up, 'grp', scatter_dimension=0, tiled=True)]
    pallas_call x0 -> x1, Pallas kernels: none -> 51 us  [local(): pl.pallas_call(functools.partial(kernel, groups, shards), out_shape=(jax....]
    all_gather x1 -> x0, blocking collectives: 25.1 us -> none  [local(): lax.all_gather(adapter_down_matrices, 'grp', axis=0, tiled=True)]
    dot_general x10 -> x0, matrix products: 22.2 us -> none  [the longest x1 5.83 us: local(): jnp.einsum('brf,bkf->brk', up_block_grads, upstream, preferred_element_ty...]
    all_gather x1 -> x0, waiting for transfers between devices: 15 us -> none  [local(): lax.all_gather(adapter_up_weight, 'grp', axis=0, tiled=True)]
  transfers between devices with their start and end apart: 4 -> 0, of which waited for: 4 -> 0; matrix products, arithmetic and copies ran while one was open for 5% -> 0% of each run, Pallas kernels for 0% -> 0%
where the time goes in v1:
time: 55.2 us; the launch traced here: 55 us
  Pallas kernels  51 us (92%)
  local copies, waits for them, and re-layouts  3.38 us (6%)
  between operations  0.64 us (1%)
    pallas_call x1, Pallas kernels, local(): pl.pallas_call(functools.partial(kernel, groups, shards), out_shape=(jax....  51 us
    unnamed x2, local copies, waits for them, and re-layouts  3.38 us

profile of v1, /device:TPU:1, one launch (start us, length us, event | category | flops | bytes accessed | tf_op | source)
XLA Modules:
  0.0 55.0 jit_solution(6655644037537829468)
XLA Ops:
  0.6 51.0 %shard_map.113 = (f32[8,16,256]{2,1,0:T(8,128)}, f32[8,16,896]{2,1,0:T(8,128)}) custom-call(bf16[4096,256]{1,0:T(8,128)(2,1)} %x_hbm.1, bf16[4096,896]{1,0:T(8,128)(2,1)} %c_hbm.1, bf16[8,16,256]{2,1,0:T(8,128)(2,1)} %ad_hbm.1, bf16[8,16,896]{2,1,0:T(8,128)(2,1)} %au_hbm.1, f32[8,16,256]{2,1,0:T(8,128)} %rd_hbm.1, f32[8,16,896]{2,1,0:T(8,128)} %ru_hbm.1, ...), custom_call_target="tpu_custom_call" | custom-call | tf_op jit(solution)/shard_map/pallas_call | solution.py:320
  51.6 1.6 %copy.14 = f32[8,16,256]{2,1,0:T(8,128)} copy(f32[8,16,256]{2,1,0:T(8,128)} %get-tuple-element.4) | data formatting | bytes 262144
  53.2 1.8 %copy.15 = f32[8,16,896]{2,1,0:T(8,128)} copy(f32[8,16,896]{2,1,0:T(8,128)} %get-tuple-element.5) | data formatting | bytes 917504

commit v2 on v1

v2 whole, which is shorter than its diff:
```python
import functools

import jax
import jax.numpy as jnp
from jax import lax
from jax.experimental import pallas as pl
from jax.experimental.pallas import tpu as pltpu
from jax.sharding import PartitionSpec as P

MESH = pl.DeviceIdType.MESH
bf16, f32, i32 = jnp.bfloat16, jnp.float32, jnp.int32
adapter_scale = 2.0


def grid_of(chips):
    across = 4 if chips % 4 == 0 else chips
    return chips // across, across


def kernel(
    groups,
    shards,
    x_hbm,
    c_hbm,
    ad_hbm,
    au_hbm,
    rd_hbm,
    ru_hbm,
    lists_hbm,
    slot_hbm,
    entry_hbm,
    rows_hbm,
    gd,
    gu,
    x,
    c,
    ad,
    au,
    rd,
    ru,
    ad_out,
    au_out,
    ad_in,
    au_in,
    mine_x,
    mine_c,
    theirs_x,
    theirs_c,
    pair_x,
    pair_c,
    rs_x,
    rs_c,
    ag_x,
    ag_c,
    spread,
    acc_d,
    acc_u,
    gd_out,
    gu_out,
    gd_in,
    gu_in,
    lists,
    slot_of,
    entry_of,
    rows_of,
    slot_tab,
    entry_tab,
    place_tab,
    load_sem,
    table_sem,
    ad_send,
    ad_recv,
    au_send,
    au_recv,
    pair_send,
    pair_recv,
    rs_send,
    rs_recv,
    ag_send,
    ag_recv,
    swap_send,
    swap_recv,
    gd_send,
    gd_recv,
    gu_send,
    gu_recv,
):
    chips = shards // 2
    high, across = grid_of(chips)
    per_owner, rank, _ = ad.shape
    listed = rd.shape[0]
    half = x.shape[0] // chips // 2
    blocks = chips // 2
    run = max(1, blocks // 2)
    me = lax.axis_index("grp")
    sh = lax.axis_index("shard")
    chip, core = lax.div(sh, 2), lax.rem(sh, 2)
    other = 1 - core
    order = sorted(range(1, groups), key=lambda d: -min(d, groups - d))

    def hops(step):
        return min(step[0], high - step[0]) + min(step[1], across - step[1])

    steps = sorted(
        ((dy, dx) for dy in range(high) for dx in range(across)), key=lambda s: -hops(s)
    )
    row, column = lax.div(chip, across), lax.rem(chip, across)
    at_step = [
        lax.rem(row + dy, high) * across + lax.rem(column + dx, across) for dy, dx in steps
    ]

    def group_at(d):
        return lax.rem(me + d, groups)

    def send(src, dst, send_sem, recv_sem, to):
        pltpu.make_async_remote_copy(
            src_ref=src,
            dst_ref=dst,
            send_sem=send_sem,
            recv_sem=recv_sem,
            device_id=to,
            device_id_type=MESH,
        ).start()

    def all_bytes(ref, sem):
        pltpu.make_async_copy(ref, ref, sem).wait()

    tables = [
        pltpu.make_async_copy(src, dst, table_sem.at[i])
        for i, (src, dst) in enumerate(
            ((lists_hbm, lists), (slot_hbm, slot_of), (entry_hbm, entry_of), (rows_hbm, rows_of))
        )
    ]
    loads = [
        pltpu.make_async_copy(src, dst, load_sem.at[i])
        for i, (src, dst) in enumerate(
            ((ad_hbm, ad), (au_hbm, au), (x_hbm, x), (c_hbm, c), (rd_hbm, rd), (ru_hbm, ru))
        )
    ]
    tables[0].start()
    tables[1].start()
    loads[0].start()

    barrier = pltpu.get_barrier_semaphore()

    def greet(to):
        pl.semaphore_signal(barrier, inc=1, device_id=to, device_id_type=MESH)

    for d in order:
        greet((group_at(d), sh))
    for b in at_step[:-1]:
        greet((me, 2 * b + core))
    greet((me, 2 * chip + other))

    loads[1].start()
    tables[2].start()
    tables[3].start()
    for load in loads[2:]:
        load.start()

    tables[0].wait()
    tables[1].wait()
    firsts = []
    for d in range(groups):
        named = group_at(d)
        first, second = i32(-1), i32(-1)
        for e in range(listed):
            s = slot_of[lists[named, e]]
            mine = lax.div(s, i32(per_owner)) == me
            at = lax.rem(s, i32(per_owner))
            second = jnp.where(mine & (first >= 0), at, second)
            first = jnp.where(mine & (first < 0), at, first)
        slot_tab[2 * d] = first
        slot_tab[2 * d + 1] = second
        firsts.append((jnp.maximum(first, 0), jnp.maximum(second, 0)))

    def pack(own, out, into):
        for d in range(groups):
            for k in range(2):
                if d:
                    out[d - 1, k] = own[firsts[d][k]]
                else:
                    into[2 * me + k] = own[firsts[d][k]]

    def send_adapters(out, into, send_sem, recv_sem):
        for d in order:
            send(
                out.at[d - 1], into.at[pl.ds(2 * me, 2)], send_sem, recv_sem, (group_at(d), sh)
            )

    loads[0].wait()
    pack(ad, ad_out, ad_in)
    pl.semaphore_wait(barrier, groups - 1 + chips)
    send_adapters(ad_out, ad_in, ad_send, ad_recv)
    loads[1].wait()
    pack(au, au_out, au_in)
    all_bytes(ad_out, ad_send)
    send_adapters(au_out, au_in, au_send, au_recv)

    owners = [lax.div(slot_of[lists[me, e]], i32(per_owner)) for e in range(listed)]
    places = []
    for e in range(listed):
        k = i32(0)
        for before in range(e):
            k = k + jnp.where(owners[before] == owners[e], 1, 0)
        places.append(2 * owners[e] + k)
        place_tab[e] = places[e]
    for p in range(2 * groups):
        found = i32(0)
        for e in range(listed):
            found = jnp.where(places[e] == p, e, found)
        entry_tab[p] = found
    tables[2].wait()
    tables[3].wait()

    def project(tokens, adapters, mine, theirs, pair, which):
        def low_of(block, out, j):
            start = pl.multiple_of(block * 2 * half, 2 * half)
            low = lax.dot_general(
                adapters[place_tab[entry_of[block]]],
                tokens[pl.ds(start, 2 * half), :],
                (((1,), (1,)), ((), ())),
                preferred_element_type=f32,
            )
            out[2 * j] = low[:, :half]
            out[2 * j + 1] = low[:, half:]

        for first in range(0, blocks, run):
            for j in range(first, first + run):
                low_of(other * blocks + j, theirs, j)
            units = pl.ds(2 * first, 2 * run)
            send(
                theirs.at[units],
                pair.at[units],
                pair_send.at[which],
                pair_recv.at[which, first // run],
                (me, 2 * chip + other),
            )
        for j in range(blocks):
            low_of(core * blocks + j, mine, j)

    def scatter(mine, pair, rs, which):
        for first in range(0, blocks, run):
            units = pl.ds(2 * first, 2 * run)
            all_bytes(pair.at[units], pair_recv.at[which, first // run])
        mine[...] += pair[...]
        for i, q in enumerate(at_step[:-1]):
            send(mine.at[q], rs.at[i], rs_send.at[which], rs_recv.at[which], (me, 2 * q + core))

    def gather(mine, rs, ag, which):
        all_bytes(rs, rs_recv.at[which])
        low = mine[chip] + jnp.sum(rs[...], axis=0)
        token = lax.rem(chip, 2) * half + lax.broadcasted_iota(i32, (rank, half), 1)
        scale = jnp.where(token < rows_of[core * blocks + lax.div(chip, 2)], adapter_scale, 0.0)
        ag[core, chip] = (low * scale).astype(bf16)
        for b in at_step[:-1]:
            unit = ag.at[core, chip]
            send(unit, unit, ag_send.at[which], ag_recv.at[which], (me, 2 * b + core))

    def swap(ag, which):
        all_bytes(ag.at[core, pl.ds(0, chips - 1)], ag_recv.at[which])
        mine = ag.at[core]
        send(mine, mine, swap_send.at[which], swap_recv.at[which], (me, 2 * chip + other))

    def place(ag, h):
        for q in range(chips):
            e = entry_of[h * blocks + q // 2]
            v = ag[h, q]
            for l in range(listed):
                spread[h, l * rank : (l + 1) * rank, q * half : (q + 1) * half] = jnp.where(
                    e == l, v, jnp.zeros_like(v)
                )

    def product(tokens, h, start, stop):
        size = chips * half
        values = tokens[pl.ds(pl.multiple_of(h * size, size), size), start:stop]
        step = jnp.dot(spread[h], values, preferred_element_type=f32)
        return step.reshape(listed, rank, stop - start)

    def gradient_own(ag, tokens, residual, acc, cuts):
        place(ag, core)
        for start, stop in cuts:
            acc[:, :, start:stop] = residual[:, :, start:stop] + product(tokens, core, start, stop)

    def gradient_rest(ag, tokens, acc, which, cuts, ready):
        all_bytes(ag.at[other], swap_recv.at[which])
        place(ag, other)
        for start, stop in cuts:
            acc[:, :, start:stop] += product(tokens, other, start, stop)
            ready(start, stop)

    def send_gradient(acc, out, into, send_sem, recv_sem, start, stop):
        for d in order:
            owner = group_at(d)
            for k in range(2):
                out[d - 1, k, :, start:stop] = acc[entry_tab[2 * owner + k], :, start:stop].astype(
                    bf16
                )
            send(
                out.at[d - 1, :, :, start:stop],
                into.at[d - 1, :, :, start:stop],
                send_sem,
                recv_sem.at[d - 1],
                (owner, sh),
            )

    def collect(acc, into, recv, total):
        values = [acc[entry_tab[2 * me + k]] for k in range(2)]
        for s in range(per_owner):
            total[s] = jnp.where(slot_tab[0] == s, values[0], 0.0) + jnp.where(
                slot_tab[1] == s, values[1], 0.0
            )
        for d in reversed(order):
            all_bytes(into.at[d - 1], recv.at[d - 1])
            values = [into[d - 1, k].astype(f32) for k in range(2)]
            at = [slot_tab[2 * (groups - d) + k] for k in range(2)]
            for s in range(per_owner):
                total[s] += jnp.where(at[0] == s, values[0], 0.0) + jnp.where(
                    at[1] == s, values[1], 0.0
                )

    wd, wu = x.shape[1], c.shape[1]
    cut = wu // 2 // 256 * 256 + 256 if wu > 512 else wu
    cuts = [(s, e) for s, e in ((0, cut), (cut, wu)) if s < e]

    loads[2].wait()
    all_bytes(ad_in.at[pl.ds(0, 2 * groups - 2)], ad_recv)
    project(x, ad_in, mine_x, theirs_x, pair_x, 0)
    scatter(mine_x, pair_x, rs_x, 0)
    gather(mine_x, rs_x, ag_x, 0)

    loads[3].wait()
    all_bytes(au_in.at[pl.ds(0, 2 * groups - 2)], au_recv)
    project(c, au_in, mine_c, theirs_c, pair_c, 1)
    swap(ag_x, 0)
    scatter(mine_c, pair_c, rs_c, 1)

    loads[5].wait()
    gradient_own(ag_x, c, ru, acc_u, cuts)
    gradient_rest(
        ag_x,
        c,
        acc_u,
        0,
        cuts,
        functools.partial(send_gradient, acc_u, gu_out, gu_in, gu_send, gu_recv),
    )

    gather(mine_c, rs_c, ag_c, 1)
    swap(ag_c, 1)
    loads[4].wait()
    gradient_own(ag_c, x, rd, acc_d, [(0, wd)])
    gradient_rest(
        ag_c,
        x,
        acc_d,
        1,
        [(0, wd)],
        functools.partial(send_gradient, acc_d, gd_out, gd_in, gd_send, gd_recv),
    )

    collect(acc_u, gu_in, gu_recv, gu)
    collect(acc_d, gd_in, gd_recv, gd)

    all_bytes(au_out, au_send)
    for which, (pair, rs, ag) in enumerate(((pair_x, rs_x, ag_x), (pair_c, rs_c, ag_c))):
        all_bytes(pair, pair_send.at[which])
        all_bytes(rs, rs_send.at[which])
        all_bytes(ag.at[0, pl.ds(0, chips - 1)], ag_send.at[which])
        all_bytes(ag.at[0], swap_send.at[which])
    all_bytes(gu_out, gu_send)
    all_bytes(gd_out, gd_send)


def solution(mesh):
    groups, shards = mesh.shape["grp"], mesh.shape["shard"]

    def local(x, c, ad, au, rd, ru, lists, slot_of, entry_of, rows_of):
        tokens, wd = x.shape
        wu = c.shape[1]
        per_owner, rank, _ = ad.shape
        listed = lists.shape[1]
        chips = shards // 2
        half = tokens // chips // 2
        vmem, smem, dma = pltpu.VMEM, pltpu.SMEM, pltpu.SemaphoreType.DMA
        places = 2 * groups
        runs = chips // 2 // max(1, chips // 4)
        return pl.pallas_call(
            functools.partial(kernel, groups, shards),
            out_shape=(vmem((per_owner, rank, wd), f32), vmem((per_owner, rank, wu), f32)),
            in_specs=[pl.BlockSpec(memory_space=pltpu.HBM)] * 10,
            out_specs=[pl.BlockSpec(memory_space=pltpu.VMEM)] * 2,
            scratch_shapes=[
                vmem((tokens, wd), bf16),
                vmem((tokens, wu), bf16),
                vmem((per_owner, rank, wd), bf16),
                vmem((per_owner, rank, wu), bf16),
                vmem((listed, rank, wd), f32),
                vmem((listed, rank, wu), f32),
                vmem((groups - 1, 2, rank, wd), bf16),
                vmem((groups - 1, 2, rank, wu), bf16),
                vmem((places, rank, wd), bf16),
                vmem((places, rank, wu), bf16),
                vmem((chips, rank, half), f32),
                vmem((chips, rank, half), f32),
                vmem((chips, rank, half), f32),
                vmem((chips, rank, half), f32),
                vmem((chips, rank, half), f32),
                vmem((chips, rank, half), f32),
                vmem((chips - 1, rank, half), f32),
                vmem((chips - 1, rank, half), f32),
                vmem((2, chips, rank, half), bf16),
                vmem((2, chips, rank, half), bf16),
                vmem((2, listed * rank, chips * half), bf16),
                vmem((listed, rank, wd), f32),
                vmem((listed, rank, wu), f32),
                vmem((groups - 1, 2, rank, wd), bf16),
                vmem((groups - 1, 2, rank, wu), bf16),
                vmem((groups - 1, 2, rank, wd), bf16),
                vmem((groups - 1, 2, rank, wu), bf16),
                smem(lists.shape, i32),
                smem(slot_of.shape, i32),
                smem(entry_of.shape, i32),
                smem(rows_of.shape, i32),
                smem((places,), i32),
                smem((places,), i32),
                smem((listed,), i32),
                dma((6,)),
                dma((4,)),
                dma,
                dma,
                dma,
                dma,
                dma((2,)),
                dma((2, runs)),
                dma((2,)),
                dma((2,)),
                dma((2,)),
                dma((2,)),
                dma((2,)),
                dma((2,)),
                dma,
                dma((groups - 1,)),
                dma,
                dma((groups - 1,)),
            ],
            compiler_params=pltpu.CompilerParams(
                collective_id=0, has_side_effects=True, vmem_limit_bytes=56 * 2**20
            ),
        )(
            x,
            c,
            ad,
            au,
            rd,
            ru,
            lists,
            slot_of,
            entry_of,
            rows_of,
        )

    split = P("grp", None, "shard")
    return jax.shard_map(
        local,
        mesh=mesh,
        in_specs=(P("grp", "shard"),) * 2 + (split,) * 4 + (P(), P(), P("grp"), P("grp")),
        out_specs=(split, split),
        check_vma=False,
    )
```

time: 55.2 us -> 48.9 us (0.89)
  Pallas kernels: 51 us -> 46.8 us
  local copies, waits for them, and re-layouts: 3.38 us -> 1.42 us
    pallas_call x1, Pallas kernels: 51 us -> 46.8 us  [local(): pl.pallas_call(functools.partial(kernel, groups, shards), out_shape=(vmem...]
    unnamed x2, local copies, waits for them, and re-layouts: 3.38 us -> 1.42 us
where the time goes in v2:
time: 48.9 us; the launch traced here: 48.8 us
  Pallas kernels  46.8 us (96%)
  local copies, waits for them, and re-layouts  1.42 us (3%)
  between operations  0.64 us (1%)
    pallas_call x1, Pallas kernels, local(): pl.pallas_call(functools.partial(kernel, groups, shards), out_shape=(vmem...  46.8 us
    unnamed x2, local copies, waits for them, and re-layouts  1.42 us

profile of v2, /device:TPU:1, one launch (start us, length us, event | category | flops | bytes accessed | tf_op | source)
XLA Modules:
  0.0 48.8 jit_solution(8138034668064369107)
XLA Ops:
  0.6 46.8 %shard_map.113 = (f32[8,16,256]{2,1,0:T(8,128)S(1)}, f32[8,16,896]{2,1,0:T(8,128)S(1)}) custom-call(bf16[4096,256]{1,0:T(8,128)(2,1)} %x_hbm.1, bf16[4096,896]{1,0:T(8,128)(2,1)} %c_hbm.1, bf16[8,16,256]{2,1,0:T(8,128)(2,1)} %ad_hbm.1, bf16[8,16,896]{2,1,0:T(8,128)(2,1)} %au_hbm.1, f32[8,16,256]{2,1,0:T(8,128)} %rd_hbm.1, f32[8,16,896]{2,1,0:T(8,128)} %ru_hbm.1, ...), custom_call_target="tpu_custom_call" | custom-call | tf_op jit(solution)/shard_map/pallas_call | solution.py:388
  47.4 0.7 %copy.14 = f32[8,16,256]{2,1,0:T(8,128)} copy(f32[8,16,256]{2,1,0:T(8,128)S(1)} %get-tuple-element.2) | data formatting | bytes 262144
  48.1 0.8 %copy.15 = f32[8,16,896]{2,1,0:T(8,128)} copy(f32[8,16,896]{2,1,0:T(8,128)S(1)} %get-tuple-element.3) | data formatting | bytes 917504

commit v3 on v2

--- a/solution.py
+++ b/solution.py
@@ -10,6 +10,11 @@
 MESH = pl.DeviceIdType.MESH
 bf16, f32, i32 = jnp.bfloat16, jnp.float32, jnp.int32
 adapter_scale = 2.0
+
+
+def cuts_of(width):
+    cut = (width // 2 // 256 + 1) * 256 if width > 512 else width // 2
+    return [(0, cut), (cut, width)]
 
 
 def grid_of(chips):
@@ -41,7 +46,8 @@
     ad_out,
     au_out,
     ad_in,
-    au_in,
+    au_in_0,
+    au_in_1,
     mine_x,
     mine_c,
     theirs_x,
@@ -97,6 +103,8 @@
     chip, core = lax.div(sh, 2), lax.rem(sh, 2)
     other = 1 - core
     order = sorted(range(1, groups), key=lambda d: -min(d, groups - d))
+    wd, wu = x.shape[1], c.shape[1]
+    cuts = cuts_of(wu)
 
     def hops(step):
         return min(step[0], high - step[0]) + min(step[1], across - step[1])
@@ -155,8 +163,6 @@
     loads[1].start()
     tables[2].start()
     tables[3].start()
-    for load in loads[2:]:
-        load.start()
 
     tables[0].wait()
     tables[1].wait()
@@ -174,28 +180,37 @@
         slot_tab[2 * d + 1] = second
         firsts.append((jnp.maximum(first, 0), jnp.maximum(second, 0)))
 
-    def pack(own, out, into):
+    def pack(own, out, parts):
         for d in range(groups):
             for k in range(2):
                 if d:
                     out[d - 1, k] = own[firsts[d][k]]
                 else:
-                    into[2 * me + k] = own[firsts[d][k]]
-
-    def send_adapters(out, into, send_sem, recv_sem):
-        for d in order:
+                    for into, (start, stop) in parts:
+                        into[2 * me + k] = own[firsts[d][k], :, start:stop]
+
+    def send_adapters(out, into, send_sem, recv_sem, turns, start, stop):
+        for d in turns:
             send(
-                out.at[d - 1], into.at[pl.ds(2 * me, 2)], send_sem, recv_sem, (group_at(d), sh)
+                out.at[d - 1, :, :, start:stop],
+                into.at[pl.ds(2 * me, 2)],
+                send_sem,
+                recv_sem,
+                (group_at(d), sh),
             )
 
     loads[0].wait()
-    pack(ad, ad_out, ad_in)
+    pack(ad, ad_out, [(ad_in, (0, wd))])
     pl.semaphore_wait(barrier, groups - 1 + chips)
-    send_adapters(ad_out, ad_in, ad_send, ad_recv)
+    send_adapters(ad_out, ad_in, ad_send, ad_recv, order, 0, wd)
+    for load in loads[2:]:
+        load.start()
     loads[1].wait()
-    pack(au, au_out, au_in)
+    au_in = (au_in_0, au_in_1)
+    pack(au, au_out, list(zip(au_in, cuts)))
     all_bytes(ad_out, ad_send)
-    send_adapters(au_out, au_in, au_send, au_recv)
+    for i, (start, stop) in enumerate(cuts):
+        send_adapters(au_out, au_in[i], au_send, au_recv.at[i], order, start, stop)
 
     owners = [lax.div(slot_of[lists[me, e]], i32(per_owner)) for e in range(listed)]
     places = []
@@ -213,29 +228,31 @@
     tables[2].wait()
     tables[3].wait()
 
-    def project(tokens, adapters, mine, theirs, pair, which):
+    def project(tokens, adapters, mine, theirs, pair, which, start, stop):
         def low_of(block, out, j):
-            start = pl.multiple_of(block * 2 * half, 2 * half)
+            first = pl.multiple_of(block * 2 * half, 2 * half)
             low = lax.dot_general(
                 adapters[place_tab[entry_of[block]]],
-                tokens[pl.ds(start, 2 * half), :],
+                tokens[pl.ds(first, 2 * half), start:stop],
                 (((1,), (1,)), ((), ())),
                 preferred_element_type=f32,
             )
-            out[2 * j] = low[:, :half]
-            out[2 * j + 1] = low[:, half:]
+            for h in range(2):
+                value = low[:, h * half : (h + 1) * half]
+                out[2 * j + h] = value if start == 0 else out[2 * j + h] + value
 
         for first in range(0, blocks, run):
             for j in range(first, first + run):
                 low_of(other * blocks + j, theirs, j)
-            units = pl.ds(2 * first, 2 * run)
-            send(
-                theirs.at[units],
-                pair.at[units],
-                pair_send.at[which],
-                pair_recv.at[which, first // run],
-                (me, 2 * chip + other),
-            )
+            if stop == tokens.shape[1]:
+                units = pl.ds(2 * first, 2 * run)
+                send(
+                    theirs.at[units],
+                    pair.at[units],
+                    pair_send.at[which],
+                    pair_recv.at[which, first // run],
+                    (me, 2 * chip + other),
+                )
         for j in range(blocks):
             low_of(core * blocks + j, mine, j)
 
@@ -282,15 +299,11 @@
         for start, stop in cuts:
             acc[:, :, start:stop] = residual[:, :, start:stop] + product(tokens, core, start, stop)
 
-    def gradient_rest(ag, tokens, acc, which, cuts, ready):
-        all_bytes(ag.at[other], swap_recv.at[which])
-        place(ag, other)
-        for start, stop in cuts:
-            acc[:, :, start:stop] += product(tokens, other, start, stop)
-            ready(start, stop)
-
-    def send_gradient(acc, out, into, send_sem, recv_sem, start, stop):
-        for d in order:
+    def gradient_rest(tokens, acc, start, stop):
+        acc[:, :, start:stop] += product(tokens, other, start, stop)
+
+    def send_gradient(acc, out, into, send_sem, recv_sem, turns, start, stop):
+        for d in turns:
             owner = group_at(d)
             for k in range(2):
                 out[d - 1, k, :, start:stop] = acc[entry_tab[2 * owner + k], :, start:stop].astype(
@@ -304,13 +317,13 @@
                 (owner, sh),
             )
 
-    def collect(acc, into, recv, total):
+    def collect(acc, into, recv, total, turns):
         values = [acc[entry_tab[2 * me + k]] for k in range(2)]
         for s in range(per_owner):
             total[s] = jnp.where(slot_tab[0] == s, values[0], 0.0) + jnp.where(
                 slot_tab[1] == s, values[1], 0.0
             )
-        for d in reversed(order):
+        for d in reversed(turns):
             all_bytes(into.at[d - 1], recv.at[d - 1])
             values = [into[d - 1, k].astype(f32) for k in range(2)]
             at = [slot_tab[2 * (groups - d) + k] for k in range(2)]
@@ -319,48 +332,40 @@
                     at[1] == s, values[1], 0.0
                 )
 
-    wd, wu = x.shape[1], c.shape[1]
-    cut = wu // 2 // 256 * 256 + 256 if wu > 512 else wu
-    cuts = [(s, e) for s, e in ((0, cut), (cut, wu)) if s < e]
-
+    arrived = pl.ds(0, 2 * groups - 2)
     loads[2].wait()
-    all_bytes(ad_in.at[pl.ds(0, 2 * groups - 2)], ad_recv)
-    project(x, ad_in, mine_x, theirs_x, pair_x, 0)
+    all_bytes(ad_in.at[arrived], ad_recv)
+    project(x, ad_in, mine_x, theirs_x, pair_x, 0, 0, wd)
     scatter(mine_x, pair_x, rs_x, 0)
     gather(mine_x, rs_x, ag_x, 0)
 
     loads[3].wait()
-    all_bytes(au_in.at[pl.ds(0, 2 * groups - 2)], au_recv)
-    project(c, au_in, mine_c, theirs_c, pair_c, 1)
+    loads[5].wait()
+    for i, (start, stop) in enumerate(cuts):
+        all_bytes(au_in[i].at[arrived], au_recv.at[i])
+        project(c, au_in[i], mine_c, theirs_c, pair_c, 1, start, stop)
+    scatter(mine_c, pair_c, rs_c, 1)
+
     swap(ag_x, 0)
-    scatter(mine_c, pair_c, rs_c, 1)
-
-    loads[5].wait()
     gradient_own(ag_x, c, ru, acc_u, cuts)
-    gradient_rest(
-        ag_x,
-        c,
-        acc_u,
-        0,
-        cuts,
-        functools.partial(send_gradient, acc_u, gu_out, gu_in, gu_send, gu_recv),
-    )
-
-    gather(mine_c, rs_c, ag_c, 1)
+    all_bytes(ag_x.at[other], swap_recv.at[0])
+    place(ag_x, other)
+    for i, (start, stop) in enumerate(cuts):
+        if i == len(cuts) - 1:
+            gather(mine_c, rs_c, ag_c, 1)
+        gradient_rest(c, acc_u, start, stop)
+        send_gradient(acc_u, gu_out, gu_in, gu_send, gu_recv, order, start, stop)
+
     swap(ag_c, 1)
     loads[4].wait()
     gradient_own(ag_c, x, rd, acc_d, [(0, wd)])
-    gradient_rest(
-        ag_c,
-        x,
-        acc_d,
-        1,
-        [(0, wd)],
-        functools.partial(send_gradient, acc_d, gd_out, gd_in, gd_send, gd_recv),
-    )
-
-    collect(acc_u, gu_in, gu_recv, gu)
-    collect(acc_d, gd_in, gd_recv, gd)
+    all_bytes(ag_c.at[other], swap_recv.at[1])
+    place(ag_c, other)
+    gradient_rest(x, acc_d, 0, wd)
+    send_gradient(acc_d, gd_out, gd_in, gd_send, gd_recv, order, 0, wd)
+
+    collect(acc_u, gu_in, gu_recv, gu, order)
+    collect(acc_d, gd_in, gd_recv, gd, order)
 
     all_bytes(au_out, au_send)
     for which, (pair, rs, ag) in enumerate(((pair_x, rs_x, ag_x), (pair_c, rs_c, ag_c))):
@@ -400,7 +405,7 @@
                 vmem((groups - 1, 2, rank, wd), bf16),
                 vmem((groups - 1, 2, rank, wu), bf16),
                 vmem((places, rank, wd), bf16),
-                vmem((places, rank, wu), bf16),
+                *(vmem((places, rank, stop - start), bf16) for start, stop in cuts_of(wu)),
                 vmem((chips, rank, half), f32),
                 vmem((chips, rank, half), f32),
                 vmem((chips, rank, half), f32),
@@ -430,7 +435,7 @@
                 dma,
                 dma,
                 dma,
-                dma,
+                dma((2,)),
                 dma((2,)),
                 dma((2, runs)),
                 dma((2,)),

time: 48.9 us -> 47.1 us (0.963)
  Pallas kernels: 46.8 us -> 44.9 us
    pallas_call x1, Pallas kernels: 46.8 us -> 44.9 us  [local(): pl.pallas_call(functools.partial(kernel, groups, shards), out_shape=(vmem...]
where the time goes in v3:
time: 47.1 us; the launch traced here: 47 us
  Pallas kernels  44.9 us (95%)
  local copies, waits for them, and re-layouts  1.42 us (3%)
  between operations  0.64 us (1%)
    pallas_call x1, Pallas kernels, local(): pl.pallas_call(functools.partial(kernel, groups, shards), out_shape=(vmem...  44.9 us
    unnamed x2, local copies, waits for them, and re-layouts  1.42 us

profile of v3, /device:TPU:1, one launch (start us, length us, event | category | flops | bytes accessed | tf_op | source)
XLA Modules:
  0.0 47.0 jit_solution(18190564238387958335)
XLA Ops:
  0.6 44.9 %shard_map.113 = (f32[8,16,256]{2,1,0:T(8,128)S(1)}, f32[8,16,896]{2,1,0:T(8,128)S(1)}) custom-call(bf16[4096,256]{1,0:T(8,128)(2,1)} %x_hbm.1, bf16[4096,896]{1,0:T(8,128)(2,1)} %c_hbm.1, bf16[8,16,256]{2,1,0:T(8,128)(2,1)} %ad_hbm.1, bf16[8,16,896]{2,1,0:T(8,128)(2,1)} %au_hbm.1, f32[8,16,256]{2,1,0:T(8,128)} %rd_hbm.1, f32[8,16,896]{2,1,0:T(8,128)} %ru_hbm.1, ...), custom_call_target="tpu_custom_call" | custom-call | tf_op jit(solution)/shard_map/pallas_call | solution.py:393
  45.5 0.7 %copy.14 = f32[8,16,256]{2,1,0:T(8,128)} copy(f32[8,16,256]{2,1,0:T(8,128)S(1)} %get-tuple-element.2) | data formatting | bytes 262144
  46.2 0.8 %copy.15 = f32[8,16,896]{2,1,0:T(8,128)} copy(f32[8,16,896]{2,1,0:T(8,128)S(1)} %get-tuple-element.3) | data formatting | bytes 917504

commit v4 on v3

--- a/solution.py
+++ b/solution.py
@@ -13,7 +13,7 @@
 
 
 def cuts_of(width):
-    cut = (width // 2 // 256 + 1) * 256 if width > 512 else width // 2
+    cut = max(width - 256, 256)
     return [(0, cut), (cut, width)]
 
 
@@ -105,6 +105,8 @@
     order = sorted(range(1, groups), key=lambda d: -min(d, groups - d))
     wd, wu = x.shape[1], c.shape[1]
     cuts = cuts_of(wu)
+    middle = (wu // 512 + 1) * 256
+    halves = [(0, middle), (middle, wu)]
 
     def hops(step):
         return min(step[0], high - step[0]) + min(step[1], across - step[1])
@@ -189,20 +191,22 @@
                     for into, (start, stop) in parts:
                         into[2 * me + k] = own[firsts[d][k], :, start:stop]
 
-    def send_adapters(out, into, send_sem, recv_sem, turns, start, stop):
-        for d in turns:
-            send(
-                out.at[d - 1, :, :, start:stop],
-                into.at[pl.ds(2 * me, 2)],
-                send_sem,
-                recv_sem,
-                (group_at(d), sh),
-            )
+    def send_adapters(out, into, send_sem, recv_sem, start, stop, pieces):
+        for k in range(0, 2, 2 // pieces):
+            n = 2 // pieces
+            for d in order:
+                send(
+                    out.at[d - 1, pl.ds(k, n), :, start:stop],
+                    into.at[pl.ds(2 * me + k, n)],
+                    send_sem,
+                    recv_sem,
+                    (group_at(d), sh),
+                )
 
     loads[0].wait()
     pack(ad, ad_out, [(ad_in, (0, wd))])
     pl.semaphore_wait(barrier, groups - 1 + chips)
-    send_adapters(ad_out, ad_in, ad_send, ad_recv, order, 0, wd)
+    send_adapters(ad_out, ad_in, ad_send, ad_recv, 0, wd, 1)
     for load in loads[2:]:
         load.start()
     loads[1].wait()
@@ -210,7 +214,7 @@
     pack(au, au_out, list(zip(au_in, cuts)))
     all_bytes(ad_out, ad_send)
     for i, (start, stop) in enumerate(cuts):
-        send_adapters(au_out, au_in[i], au_send, au_recv.at[i], order, start, stop)
+        send_adapters(au_out, au_in[i], au_send, au_recv.at[i], start, stop, 2 - i)
 
     owners = [lax.div(slot_of[lists[me, e]], i32(per_owner)) for e in range(listed)]
     places = []
@@ -347,11 +351,11 @@
     scatter(mine_c, pair_c, rs_c, 1)
 
     swap(ag_x, 0)
-    gradient_own(ag_x, c, ru, acc_u, cuts)
+    gradient_own(ag_x, c, ru, acc_u, halves)
     all_bytes(ag_x.at[other], swap_recv.at[0])
     place(ag_x, other)
-    for i, (start, stop) in enumerate(cuts):
-        if i == len(cuts) - 1:
+    for i, (start, stop) in enumerate(halves):
+        if i == len(halves) - 1:
             gather(mine_c, rs_c, ag_c, 1)
         gradient_rest(c, acc_u, start, stop)
         send_gradient(acc_u, gu_out, gu_in, gu_send, gu_recv, order, start, stop)

time: 47.1 us -> 46.3 us (0.983)
  Pallas kernels: 44.9 us -> 44.2 us
    pallas_call x1, Pallas kernels: 44.9 us -> 44.2 us  [local(): pl.pallas_call(functools.partial(kernel, groups, shards), out_shape=(vmem...]
where the time goes in v4:
time: 46.3 us; the launch traced here: 46.2 us
  Pallas kernels  44.2 us (95%)
  local copies, waits for them, and re-layouts  1.42 us (3%)
  between operations  0.64 us (1%)
    pallas_call x1, Pallas kernels, local(): pl.pallas_call(functools.partial(kernel, groups, shards), out_shape=(vmem...  44.2 us
    unnamed x2, local copies, waits for them, and re-layouts  1.42 us

profile of v4, /device:TPU:1, one launch (start us, length us, event | category | flops | bytes accessed | tf_op | source)
XLA Modules:
  0.0 46.2 jit_solution(15088534711667580893)
XLA Ops:
  0.6 44.2 %shard_map.113 = (f32[8,16,256]{2,1,0:T(8,128)S(1)}, f32[8,16,896]{2,1,0:T(8,128)S(1)}) custom-call(bf16[4096,256]{1,0:T(8,128)(2,1)} %x_hbm.1, bf16[4096,896]{1,0:T(8,128)(2,1)} %c_hbm.1, bf16[8,16,256]{2,1,0:T(8,128)(2,1)} %ad_hbm.1, bf16[8,16,896]{2,1,0:T(8,128)(2,1)} %au_hbm.1, f32[8,16,256]{2,1,0:T(8,128)} %rd_hbm.1, f32[8,16,896]{2,1,0:T(8,128)} %ru_hbm.1, ...), custom_call_target="tpu_custom_call" | custom-call | tf_op jit(solution)/shard_map/pallas_call | solution.py:397
  44.8 0.7 %copy.14 = f32[8,16,256]{2,1,0:T(8,128)} copy(f32[8,16,256]{2,1,0:T(8,128)S(1)} %get-tuple-element.2) | data formatting | bytes 262144
  45.5 0.8 %copy.15 = f32[8,16,896]{2,1,0:T(8,128)} copy(f32[8,16,896]{2,1,0:T(8,128)S(1)} %get-tuple-element.3) | data formatting | bytes 917504

commit v5 on v4

--- a/solution.py
+++ b/solution.py
@@ -147,10 +147,6 @@
             ((ad_hbm, ad), (au_hbm, au), (x_hbm, x), (c_hbm, c), (rd_hbm, rd), (ru_hbm, ru))
         )
     ]
-    tables[0].start()
-    tables[1].start()
-    loads[0].start()
-
     barrier = pltpu.get_barrier_semaphore()
 
     def greet(to):
@@ -162,6 +158,9 @@
         greet((me, 2 * b + core))
     greet((me, 2 * chip + other))
 
+    tables[0].start()
+    tables[1].start()
+    loads[0].start()
     loads[1].start()
     tables[2].start()
     tables[3].start()

time: 46.3 us -> 46.3 us (level)
  no operation moved by 1% of the time
where the time goes in v5:
time: 46.3 us; the launch traced here: 46.2 us
  Pallas kernels  44.2 us (95%)
  local copies, waits for them, and re-layouts  1.42 us (3%)
  between operations  0.64 us (1%)
    pallas_call x1, Pallas kernels, local(): pl.pallas_call(functools.partial(kernel, groups, shards), out_shape=(vmem...  44.2 us
    unnamed x2, local copies, waits for them, and re-layouts  1.42 us

profile of v5, /device:TPU:1, one launch (start us, length us, event | category | flops | bytes accessed | tf_op | source)
XLA Modules:
  0.0 46.2 jit_solution(1436652300863195148)
XLA Ops:
  0.6 44.2 %shard_map.113 = (f32[8,16,256]{2,1,0:T(8,128)S(1)}, f32[8,16,896]{2,1,0:T(8,128)S(1)}) custom-call(bf16[4096,256]{1,0:T(8,128)(2,1)} %x_hbm.1, bf16[4096,896]{1,0:T(8,128)(2,1)} %c_hbm.1, bf16[8,16,256]{2,1,0:T(8,128)(2,1)} %ad_hbm.1, bf16[8,16,896]{2,1,0:T(8,128)(2,1)} %au_hbm.1, f32[8,16,256]{2,1,0:T(8,128)} %rd_hbm.1, f32[8,16,896]{2,1,0:T(8,128)} %ru_hbm.1, ...), custom_call_target="tpu_custom_call" | custom-call | tf_op jit(solution)/shard_map/pallas_call | solution.py:396
  44.8 0.7 %copy.14 = f32[8,16,256]{2,1,0:T(8,128)} copy(f32[8,16,256]{2,1,0:T(8,128)S(1)} %get-tuple-element.2) | data formatting | bytes 262144
  45.5 0.8 %copy.15 = f32[8,16,896]{2,1,0:T(8,128)} copy(f32[8,16,896]{2,1,0:T(8,128)S(1)} %get-tuple-element.3) | data formatting | bytes 917504
